TPU v7x, 512 devices: a whole 4x4x16 slice. The times are simulated.
512 devices in a mesh: rows: 8 (over z_lo), chan: 64 (over y, x, z_hi, core).
Axes of the slice: x: 4, y: 4, z: 16 (z_hi: 2, z_lo: 8; z = z_hi * 8 + z_lo), core: 2. Of those that a mesh axis runs over, the one named last changes fastest.
Arguments:
- activations: bfloat16 [256, 7, 7, 512], P('rows', None, None, 'chan'), may hold values from 0 to 2
- cotangents: bfloat16 [256, 512, 49], P('rows', 'chan'), may hold values from -0.0005859375 to 0.0005859375
- ordering: int32 [8, 32], P('rows'), may hold values from 0 to 31, each once within a row
- ridge: float32 [128], replicated, may hold values from 0.2 to 2
Outputs:
- gram_panel: float32 [256, 128], P('rows')
- factor_panel: float32 [256, 128], P('rows')
Inputs may be any that keep to these rules, and one draw needn't show every extreme that they name: Each row of ordering lists every one of the group's 32 examples once.
All inputs are finite; a program needn't handle non-finite values.
Results may differ from a plain program's by a relative error of at most 0.0003.
Values may be sent and summed in bfloat16 or wider, within the bound.
A program may use at most 64 MiB of HBM per device.

v0:
```python
import jax
import jax.numpy as jnp
from jax import lax
from jax.sharding import PartitionSpec as P

PIV_DEV = 16


def jacobian_block(grad_rows, input_rows):
    example_count = input_rows.shape[0]
    side_len = input_rows.shape[1]
    channel_count = input_rows.shape[3]
    grad_count = grad_rows.shape[1]
    grid_grads = grad_rows.reshape(example_count, grad_count, side_len, side_len)
    padded_grads = jnp.pad(grid_grads, ((0, 0), (0, 0), (1, 1), (1, 1)))
    shifted = []
    for row_shift in range(3):
        for col_shift in range(3):
            window = padded_grads[
                :,
                :,
                2 - row_shift : 2 - row_shift + side_len,
                2 - col_shift : 2 - col_shift + side_len,
            ]
            shifted.append(window.reshape(example_count, grad_count, side_len * side_len))
    stacked_grads = jnp.stack(shifted, axis=2).reshape(
        example_count, grad_count * 9, side_len * side_len
    )
    flat_inputs = input_rows.reshape(example_count, side_len * side_len, channel_count)
    product = jnp.einsum(
        "nkp,npq->nkq", stacked_grads, flat_inputs, preferred_element_type=jnp.float32
    )
    return product.astype(jnp.bfloat16).reshape(example_count, -1)


def gram_block(left_rows, right_rows):
    return lax.dot_general(
        left_rows, right_rows, (((1,), (1,)), ((), ())), preferred_element_type=jnp.float32
    )


def local(activations, cotangents, ordering, ridge):
    local_order = ordering[0]
    own_inputs = jnp.take(activations, local_order, axis=0)
    own_grads = jnp.take(cotangents, local_order, axis=0)
    pivot_count = PIV_DEV
    pivot_inputs, pivot_grads = (
        lax.all_gather(own_inputs[:pivot_count], "rows", axis=0, tiled=True),
        lax.all_gather(own_grads[:pivot_count], "rows", axis=0, tiled=True),
    )
    full_own, full_pivot = (
        lax.all_gather(own_inputs, "chan", axis=3, tiled=True),
        lax.all_gather(pivot_inputs, "chan", axis=3, tiled=True),
    )
    own_jac = jacobian_block(own_grads, full_own)
    pivot_jac = jacobian_block(pivot_grads, full_pivot)
    partial_panel = gram_block(own_jac, pivot_jac)
    gram_panel = lax.psum(partial_panel, "chan")
    diag_block = lax.all_gather(gram_panel[:pivot_count], "rows", axis=0, tiled=True)
    system = 0.5 * (diag_block + diag_block.T) + jnp.diag(ridge)
    lower = jnp.linalg.cholesky(system)
    factor_panel = jax.scipy.linalg.solve_triangular(lower, gram_panel.T, lower=True).T
    return (gram_panel, factor_panel)


def solution(mesh):
    return jax.shard_map(
        local,
        mesh=mesh,
        in_specs=(P("rows", None, None, "chan"), P("rows", "chan", None), P("rows", None), P()),
        out_specs=(P("rows", None), P("rows", None)),
        check_vma=False,
    )
```

profile of v0, /device:TPU:32, one launch (start us, length us, event | category | flops | bytes accessed | tf_op | source)
XLA Modules:
  0.0 1040.8 jit_solution(938271558096505673)
XLA Ops:
  7.2 0.0 all-gather.3.cloned.1.call-start
  7.2 0.7 fusion.16
  7.9 0.7 compare_and_fusion
  8.6 1.2 copy.86
  9.8 0.6 gather_fusion.1
  10.4 0.1 broadcast_select_fusion
  10.5 0.9 copy.87
  11.5 0.0 all-gather.3.cloned.1.call-update
  11.5 0.0 all-gather.5.cloned.1.call-start
  11.6 61.5 %all_gather.17 = bf16[128,7,7,8]{3,2,1,0:T(8,128)(2,1)S(1)} all-gather(bf16[16,7,7,8]{3,2,1,0:T(8,128)(2,1)S(1)} %slice.96), channel_id=1, replica_groups=mesh['rows'=8,'chan'=64] {'rows'}, dimensions={0}, use_global_device_ids=true | all-gather | bytes 112896 | tf_op jit(solution)/shard_map/all_gather | solution.py:48
  73.1 2.7 copy.94
  75.8 0.0 all-gather.5.cloned.1.call-update
  75.8 0.6 gather_fusion
  76.4 0.2 copy.76
  76.6 0.1 slice_select_fusion
  76.7 89.2 %all_gather.16 = bf16[128,8,49]{2,1,0:T(8,128)(2,1)S(1)} all-gather(bf16[16,8,49]{2,1,0:T(8,128)(2,1)S(1)} %slice_select_fusion), channel_id=1, replica_groups=mesh['rows'=8,'chan'=64] {'rows'}, dimensions={0}, use_global_device_ids=true | all-gather | bytes 112896 | tf_op jit(solution)/shard_map/all_gather | solution.py:49
  165.8 0.2 copy.91
  166.1 0.1 pad_slice_fusion
  166.4 0.1 copy.93
  166.5 2.0 copy.96
  168.6 0.1 pad_slice_fusion.8
  168.7 0.2 copy.77
  168.9 0.2 copy.78
  169.0 0.2 copy.79
  169.2 0.2 copy.80
  169.3 0.2 copy.81
  169.5 0.2 copy.82
  169.7 0.2 copy.83
  169.8 0.2 copy.84
  170.1 0.1 fusion.15
  170.3 0.1 copy.85
  170.4 26.6 %all-gather.3.cloned.1.call-done = bf16[32,7,7,512]{0,3,2,1:T(8,128)(2,1)} async-done(((bf16[32,7,7,8]{0,3,2,1:T(8,128)(2,1)}), bf16[32,7,7,512]{0,3,2,1:T(8,128)(2,1)}) %all-gather.3.cloned.1.call-update) | async-done | bytes 1605648 | tf_op jit(solution)/shard_map/all_gather | solution.py:52
  196.9 7.6 copy.90
  204.5 3.8 convolution_convert_fusion.1
  208.3 162.3 %all-gather.5.cloned.1.call-done = bf16[128,7,7,512]{0,3,2,1:T(8,128)(2,1)} async-done(((bf16[128,7,7,8]{0,3,2,1:T(8,128)(2,1)}), bf16[128,7,7,512]{0,3,2,1:T(8,128)(2,1)}) %all-gather.5.cloned.1.call-update) | async-done | bytes 6422544 | tf_op jit(solution)/shard_map/all_gather | solution.py:53
  370.5 11.8 %copy.97 = bf16[128,49,512]{2,1,0:T(8,128)(2,1)} copy(bf16[128,49,512]{0,2,1:T(8,128)(2,1)} %bitcast.73) | data formatting | bytes 12845056 | tf_op jit(solution)/shard_map/reshape | solution.py:29
  382.3 5.9 convolution_convert_fusion
  388.2 9.4 fusion.3
  397.6 559.4 %psum.7 = f32[32,128]{1,0:T(8,128)S(1)} all-reduce(f32[32,128]{1,0:T(8,128)S(1)} %fusion.3), channel_id=1, replica_groups=mesh['rows'=8,'chan'=64] {'chan'}, use_global_device_ids=true, to_apply=%region_0.1 | all-reduce | flops 4096 | bytes 32768 | tf_op jit(solution)/shard_map/psum | solution.py:58
  957.0 53.0 %all_gather.19 = f32[128,128]{1,0:T(8,128)S(1)} all-gather(f32[16,128]{1,0:T(8,128)S(1)} %slice.97), channel_id=1, replica_groups=mesh['rows'=8,'chan'=64] {'rows'}, dimensions={0}, use_global_device_ids=true | all-gather | bytes 73728 | tf_op jit(solution)/shard_map/all_gather | solution.py:59
  1010.0 0.1 copy.100
  1010.1 0.1 fusion.14
  1010.2 0.1 copy.101
  1010.3 11.7 %cholesky.16 = f32[128,128]{1,0:T(8,128)S(1)} custom-call(f32[128,128]{1,0:T(8,128)S(1)} %fusion.12), custom_call_target="Cholesky" | custom-call | tf_op jit(solution)/shard_map/jit(cholesky)/cholesky | solution.py:61
  1022.0 0.6 compare_reduce_fusion
  1022.7 0.7 fusion.9
  1023.3 9.8 custom-call.7
  1033.2 0.8 fusion.10
  (29 shorter events, 0.4 us)
Async XLA Ops:
  7.2 68.7 %copy-start = (bf16[32,8,49]{2,1,0:T(8,128)(2,1)S(1)}, bf16[32,8,49]{2,1,0:T(8,128)(2,1)}, u32[]{:S(2)}) copy-start(bf16[32,8,49]{2,1,0:T(8,128)(2,1)} %param.5) | copy-start | bytes 75268
  7.2 189.8 %all-gather.3.cloned.1.call-start = ((), (), s32[]{:S(2)}) async-start(), calls=%async_computation | async-start | bytes 6522880 | tf_op jit(solution)/shard_map/all_gather | solution.py:52
  11.5 359.1 %all-gather.5.cloned.1.call-start = ((), (), s32[]{:S(2)}) async-start(), calls=%async_computation.1 | async-start | bytes 6522880 | tf_op jit(solution)/shard_map/all_gather | solution.py:53
  388.2 621.9 %copy-start.2 = (f32[128]{0:T(128)S(1)}, f32[128]{0:T(128)}, u32[]{:S(2)}) copy-start(f32[128]{0:T(128)} %param.7) | copy-start | bytes 1540
  957.0 77.0 %copy-start.1 = (f32[32,128]{1,0:T(8,128)}, f32[32,128]{1,0:T(8,128)S(1)}, u32[]{:S(2)}) copy-start(f32[32,128]{1,0:T(8,128)S(1)} %psum.7) | copy-start | bytes 49156
Sparse Core Ops, SparseCore 0:
  12.2 184.6 all-gather.2
  201.1 169.3 all-gather.4
where the time goes:
time: 1040 us
  blocking collectives  763 us (73%)
  waiting for transfers between devices  189 us (18%)
  local copies, waits for them, and re-layouts  30 us (3%)
  other arithmetic  24.6 us (2%)
  matrix products  19.8 us (2%)
  between operations  14.3 us (1%)
    psum x1, blocking collectives, local(): gram_panel = lax.psum(partial_panel, 'chan')  559 us
    all_gather x1, waiting for transfers between devices, local(): lax.all_gather(pivot_inputs, 'chan', axis=3, tiled=True)  162 us
    all_gather x1, blocking collectives, local(): lax.all_gather(own_grads[:pivot_count], 'rows', axis=0, tiled=True)  89.2 us
    all_gather x1, blocking collectives, local(): lax.all_gather(own_inputs[:pivot_count], 'rows', axis=0, tiled=True)  61.5 us
    all_gather x1, blocking collectives, local(): lax.all_gather(gram_panel[:pivot_count], 'rows', axis=0, tiled=True)  53 us
    all_gather x1, waiting for transfers between devices, local(): lax.all_gather(own_inputs, 'chan', axis=3, tiled=True)  26.6 us
  transfers between devices with their start and end apart: 2, of which 2 were waited for; matrix products, arithmetic and copies ran while one was open for 2% of the time, Pallas kernels for 0%

commit v1 on v0

--- a/solution.py
+++ b/solution.py
@@ -55,7 +55,7 @@
     own_jac = jacobian_block(own_grads, full_own)
     pivot_jac = jacobian_block(pivot_grads, full_pivot)
     partial_panel = gram_block(own_jac, pivot_jac)
-    gram_panel = lax.psum(partial_panel, "chan")
+    gram_panel = jnp.sum(lax.all_gather(partial_panel, "chan"), axis=0)
     diag_block = lax.all_gather(gram_panel[:pivot_count], "rows", axis=0, tiled=True)
     system = 0.5 * (diag_block + diag_block.T) + jnp.diag(ridge)
     lower = jnp.linalg.cholesky(system)

time: 1040 us -> 584 us (0.56)
  the two profiles are of different devices: /device:TPU:32 before, /device:TPU:2 now
where the time goes in v1:
time: 584 us; the launch traced here: 583 us
  waiting for transfers between devices  324 us (55%)
  blocking collectives  169 us (29%)
  local copies, waits for them, and re-layouts  30 us (5%)
  other arithmetic  25.9 us (4%)
  matrix products  20.4 us (3%)
  between operations  14.1 us (2%)
    all_gather x1, waiting for transfers between devices, local(): lax.all_gather(pivot_inputs, 'chan', axis=3, tiled=True)  159 us
    all_gather x1, waiting for transfers between devices, local(): gram_panel = jnp.sum(lax.all_gather(partial_panel, 'chan'), axis=0)  102 us
    all_gather x1, blocking collectives, local(): lax.all_gather(own_inputs[:pivot_count], 'rows', axis=0, tiled=True)  62.2 us
    all_gather x1, waiting for transfers between devices, local(): lax.all_gather(own_inputs, 'chan', axis=3, tiled=True)  62.1 us
    all_gather x1, blocking collectives, local(): lax.all_gather(own_grads[:pivot_count], 'rows', axis=0, tiled=True)  60 us
    all_gather x1, blocking collectives, local(): lax.all_gather(gram_panel[:pivot_count], 'rows', axis=0, tiled=True)  46.4 us
    reshape x2, local copies, waits for them, and re-layouts, jacobian_block(): input_rows.reshape(example_count, side_len * side_len, channel_count)  19.3 us
    another operation x3, other arithmetic, local(): lower = jnp.linalg.cholesky(system)  12.4 us
  transfers between devices with their start and end apart: 3, of which 3 were waited for; matrix products, arithmetic and copies ran while one was open for 3% of the time, Pallas kernels for 0%

profile of v1, /device:TPU:2, one launch (start us, length us, event | category | flops | bytes accessed | tf_op | source)
XLA Modules:
  0.0 583.0 jit_solution(5860880630565171277)
XLA Ops:
  7.2 0.0 all-gather.5.cloned.1.call-start
  7.2 0.7 fusion.16
  7.9 0.7 compare_and_fusion
  8.6 1.2 copy.83
  9.8 0.6 gather_fusion.1
  10.4 0.1 broadcast_select_fusion
  10.5 0.9 copy.84
  11.5 0.0 all-gather.7.cloned.1.call-start
  11.6 62.2 %all_gather.23 = bf16[128,7,7,8]{3,2,1,0:T(8,128)(2,1)S(1)} all-gather(bf16[16,7,7,8]{3,2,1,0:T(8,128)(2,1)S(1)} %slice.96), channel_id=1, replica_groups=mesh['rows'=8,'chan'=64] {'rows'}, dimensions={0}, use_global_device_ids=true | all-gather | bytes 112896 | tf_op jit(solution)/shard_map/all_gather | solution.py:48
  73.8 2.7 copy.91
  76.5 0.0 all-gather.9.cloned.1.call-start
  76.6 0.6 gather_fusion
  77.2 0.2 copy.73
  77.3 0.1 slice_select_fusion
  77.4 60.0 %all_gather.22 = bf16[128,8,49]{2,1,0:T(8,128)(2,1)S(1)} all-gather(bf16[16,8,49]{2,1,0:T(8,128)(2,1)S(1)} %slice_select_fusion), channel_id=1, replica_groups=mesh['rows'=8,'chan'=64] {'rows'}, dimensions={0}, use_global_device_ids=true | all-gather | bytes 112896 | tf_op jit(solution)/shard_map/all_gather | solution.py:49
  137.4 0.2 copy.88
  137.7 0.1 pad_slice_fusion
  138.0 0.1 copy.90
  138.1 2.0 copy.93
  140.2 0.1 pad_slice_fusion.8
  140.3 0.2 copy.74
  140.5 0.2 copy.75
  140.6 0.2 copy.76
  140.8 0.2 copy.77
  140.9 0.2 copy.78
  141.1 0.2 copy.79
  141.3 0.2 copy.80
  141.4 0.2 copy.81
  141.7 0.1 fusion.15
  141.9 0.1 copy.82
  142.0 62.1 %all-gather.5.cloned.1.call-done = bf16[32,7,7,512]{0,3,2,1:T(8,128)(2,1)} async-done(((bf16[32,7,7,8]{0,3,2,1:T(8,128)(2,1)}), bf16[32,7,7,512]{0,3,2,1:T(8,128)(2,1)}) %all-gather.5.cloned.1.call-update) | async-done | bytes 1605648 | tf_op jit(solution)/shard_map/all_gather | solution.py:52
  204.0 7.5 %copy.87 = bf16[32,49,512]{2,1,0:T(8,128)(2,1)} copy(bf16[32,49,512]{0,2,1:T(8,128)(2,1)} %bitcast.73) | data formatting | bytes 3211264 | tf_op jit(solution)/shard_map/reshape | solution.py:29
  211.6 3.8 convolution_convert_fusion.1
  215.3 159.4 %all-gather.7.cloned.1.call-done = bf16[128,7,7,512]{0,3,2,1:T(8,128)(2,1)} async-done(((bf16[128,7,7,8]{0,3,2,1:T(8,128)(2,1)}), bf16[128,7,7,512]{0,3,2,1:T(8,128)(2,1)}) %all-gather.7.cloned.1.call-update) | async-done | bytes 6422544 | tf_op jit(solution)/shard_map/all_gather | solution.py:53
  374.7 11.8 %copy.94 = bf16[128,49,512]{2,1,0:T(8,128)(2,1)} copy(bf16[128,49,512]{0,2,1:T(8,128)(2,1)} %bitcast.74) | data formatting | bytes 12845056 | tf_op jit(solution)/shard_map/reshape | solution.py:29
  386.5 5.9 %convolution_convert_fusion = bf16[128,72,512]{2,1,0:T(8,128)(2,1)S(1)} fusion(bf16[128,72,49]{1,2,0:T(8,128)(2,1)S(1)} %copy.93, bf16[128,49,512]{2,1,0:T(8,128)(2,1)} %copy.94), kind=kOutput, calls=%fused_computation.4 | convolution fusion | flops 467140608 | bytes 16762880 | tf_op jit(solution)/shard_map/nkp,npq->nkq/dot_general | solution.py:30
  392.4 10.0 %fusion.3 = f32[32,128]{1,0:T(8,128)} fusion(bf16[128,72,512]{2,1,0:T(8,128)(2,1)S(1)} %convolution_convert_fusion, bf16[32,72,512]{2,1,0:T(8,128)(2,1)} %convolution_convert_fusion.1), kind=kOutput, calls=%fused_computation.7 | convolution fusion | flops 301989888 | bytes 11812864 | tf_op jit(solution)/shard_map/dot_general | solution.py:37
  402.5 102.3 %all-gather.9.cloned.1.call-done = f32[2048,128]{1,0:T(8,128)} async-done(((f32[32,128]{1,0:T(8,128)}), f32[2048,128]{1,0:T(8,128)}) %all-gather.9.cloned.1.call-update) | async-done | bytes 1048592 | tf_op jit(solution)/shard_map/all_gather | solution.py:58
  504.7 1.3 reduce_sum.9
  506.1 46.4 %all_gather.27 = f32[128,128]{1,0:T(8,128)S(1)} all-gather(f32[16,128]{1,0:T(8,128)S(1)} %slice.97), channel_id=1, replica_groups=mesh['rows'=8,'chan'=64] {'rows'}, dimensions={0}, use_global_device_ids=true | all-gather | bytes 73728 | tf_op jit(solution)/shard_map/all_gather | solution.py:59
  552.5 0.1 copy.97
  552.6 0.1 fusion.14
  552.7 0.1 copy.98
  552.8 11.7 %cholesky.16 = f32[128,128]{1,0:T(8,128)S(1)} custom-call(f32[128,128]{1,0:T(8,128)S(1)} %fusion.12), custom_call_target="Cholesky" | custom-call | tf_op jit(solution)/shard_map/jit(cholesky)/cholesky | solution.py:61
  564.5 0.6 compare_reduce_fusion
  565.2 0.7 fusion.9
  565.8 9.8 %custom-call.7 = f32[1,128,128]{1,2,0:T(8,128)S(1)} custom-call(f32[1,128,128]{2,1,0:T(8,128)S(1)} %fusion.9), custom_call_target="InvertDiagBlocksLowerTriangular" | custom-call | tf_op jit(solution)/shard_map/jit(_solve_triangular)/triangular_solve | solution.py:62
  575.6 0.8 fusion.10
  (32 shorter events, 0.4 us)
Async XLA Ops:
  7.2 69.4 %copy-start = (bf16[32,8,49]{2,1,0:T(8,128)(2,1)S(1)}, bf16[32,8,49]{2,1,0:T(8,128)(2,1)}, u32[]{:S(2)}) copy-start(bf16[32,8,49]{2,1,0:T(8,128)(2,1)} %param.5) | copy-start | bytes 75268
  7.2 196.8 %all-gather.5.cloned.1.call-start = ((), (), s32[]{:S(2)}) async-start(), calls=%async_computation | async-start | bytes 6522880 | tf_op jit(solution)/shard_map/all_gather | solution.py:52
  11.5 363.2 %all-gather.7.cloned.1.call-start = ((), (), s32[]{:S(2)}) async-start(), calls=%async_computation.1 | async-start | bytes 6522880 | tf_op jit(solution)/shard_map/all_gather | solution.py:53
  76.5 428.2 %all-gather.9.cloned.1.call-start = ((), (), s32[]{:S(2)}) async-start(), calls=%async_computation.2 | async-start | bytes 1064960 | tf_op jit(solution)/shard_map/all_gather | solution.py:58
  392.4 160.2 %copy-start.2 = (f32[128]{0:T(128)S(1)}, f32[128]{0:T(128)}, u32[]{:S(2)}) copy-start(f32[128]{0:T(128)} %param.7) | copy-start | bytes 1540
  506.1 70.4 %copy-start.1 = (f32[32,128]{1,0:T(8,128)}, f32[32,128]{1,0:T(8,128)S(1)}, u32[]{:S(2)}) copy-start(f32[32,128]{1,0:T(8,128)S(1)} %reduce_sum.9) | copy-start | bytes 49156
Sparse Core Ops, SparseCore 0:
  12.2 191.7 all-gather.4
  208.2 166.4 all-gather.6
  402.6 102.0 all-gather.8
